TPU v7x, 32 devices: a whole 2x2x4 slice. The times are simulated.
32 devices in a mesh: fsdp: 8 (over z, y), rep: 4 (over x, core).
Axes of the slice: x: 2, y: 2, z: 4, core: 2. Of those that a mesh axis runs over, the one named last changes fastest.
Arguments:
- tokens: bfloat16 [8192, 1088], P(('fsdp', 'rep')), may hold values from -6 to 6
- lengths: int32 [32, 4], P(('fsdp', 'rep')), may hold values from 0 to 256, as said below
- attn_weights: bfloat16 [4352, 1088], P(('fsdp', 'rep'))
- vectors: bfloat16 [13056], P(('fsdp', 'rep'))
- up_weights: bfloat16 [4352, 1088], P(('fsdp', 'rep')), may hold values from -0.1875 to 0.1875
- down_weights: bfloat16 [4352, 1088], P(('fsdp', 'rep')), may hold values from -0.09375 to 0.09375
- cotangent: bfloat16 [8192, 1088], P(('fsdp', 'rep')), may hold values from -6 to 6
Outputs:
- out: bfloat16 [8192, 1088], P(('fsdp', 'rep'))
- grad_tokens: bfloat16 [8192, 1088], P(('fsdp', 'rep'))
- grad_attn_weights: float32 [4352, 1088], P(('fsdp', 'rep'))
- grad_vectors: float32 [13056], P(('fsdp', 'rep'))
- grad_up_weights: float32 [4352, 1088], P(('fsdp', 'rep'))
- grad_down_weights: float32 [4352, 1088], P(('fsdp', 'rep'))
Inputs may be any that keep to these rules, and one draw needn't show every extreme that they name: `lengths`: row p gives, in order from slot 0, the sequences packed into the blocks of pack p, which is held by device p of fsdp+rep (fsdp major); a row sums to at most 256 and the slots after its sum are empty; in every draw one row, drawn from the seed, is a single sequence of 256 tokens followed by zeros.
All inputs are finite; a program needn't handle non-finite values.
Results may differ from a plain program's by a relative error of at most 0.013.
Values may be sent and summed in bfloat16 or wider, within the bound.
A program may use at most 192 MiB of HBM per device.

v0:
```python
import jax
import jax.numpy as jnp
from jax import lax
from jax.sharding import PartitionSpec as P

HEADS = 17
HEAD_DIM = 64
FF = 4352
epsilon = 1e-05
negative = -1e30


def for_sending(shard):
    return jax.tree.map(lambda a: a.astype(jnp.bfloat16) if a.dtype == jnp.float32 else a, shard)


def contract(left, right, left_dim, right_dim):
    return lax.dot_general(
        left, right, (((left_dim,), (right_dim,)), ((), ())), preferred_element_type=jnp.float32
    )


def normalize(values):
    center = values - jnp.mean(values, axis=1, keepdims=True)
    scaled = lax.rsqrt(jnp.mean(center * center, axis=1, keepdims=True) + epsilon)
    return (center * scaled, scaled)


def norm_back(grad_normed, normed, scaled, gain):
    scaled_grad = grad_normed * gain
    return scaled * (
        scaled_grad
        - jnp.mean(scaled_grad, axis=1, keepdims=True)
        - normed * jnp.mean(scaled_grad * normed, axis=1, keepdims=True)
    )


def visible(segment, span_rows):
    row_ids = lax.iota(jnp.int32, span_rows)[:, None]
    col_ids = lax.iota(jnp.int32, segment.shape[0])[None, :]
    same_seg = segment[:, None] == segment[None, :]
    return same_seg & (col_ids <= row_ids)


def split_heads(matrix):
    return matrix.reshape(matrix.shape[0], HEADS, HEAD_DIM).transpose(1, 0, 2)


def join_heads(stacked):
    return stacked.transpose(1, 0, 2).reshape(stacked.shape[1], HEADS * HEAD_DIM)


def by_owner(matrix, outer_count, inner_count):
    slot_count, width = matrix.shape
    block_width = width // (outer_count * inner_count)
    return matrix.reshape(slot_count, outer_count, inner_count, block_width).transpose(0, 2, 1, 3)


def head_forward(head_parts, segment, span_rows):
    queries, key_heads, value_heads = head_parts
    factor = HEAD_DIM ** (-0.5)
    allowed = visible(segment, span_rows)
    raw_scores = contract(queries, key_heads, 1, 1)
    scores = jnp.where(allowed, raw_scores * factor, negative)
    row_peak = jnp.max(scores, axis=1, keepdims=True)
    exp_scores = jnp.exp(scores - row_peak)
    row_total = jnp.sum(exp_scores, axis=1, keepdims=True)
    prob_low = (exp_scores / row_total).astype(jnp.bfloat16)
    outputs = [contract(prob_low, value_heads, 1, 0)]
    totals = [row_peak + jnp.log(row_total)]
    return (jnp.concatenate(outputs, axis=0).astype(jnp.bfloat16), jnp.concatenate(totals, axis=0))


def head_backward(head_parts, segment, span_rows):
    queries, key_heads, value_heads, totals, grad_mixed = head_parts
    factor = HEAD_DIM ** (-0.5)
    grad_keys = jnp.zeros(key_heads.shape, jnp.float32)
    grad_values = jnp.zeros(value_heads.shape, jnp.float32)
    allowed = visible(segment, span_rows)
    grad_rows = grad_mixed[0:span_rows]
    raw_scores = contract(queries, key_heads, 1, 1)
    probs = jnp.where(allowed, jnp.exp(raw_scores * factor - totals[0:span_rows]), 0.0)
    grad_probs = contract(grad_rows, value_heads, 1, 1)
    row_delta = jnp.sum(probs * grad_probs, axis=1, keepdims=True)
    grad_scores = (probs * (grad_probs - row_delta) * factor).astype(jnp.bfloat16)
    grad_queries = [contract(grad_scores, key_heads, 1, 0)]
    grad_keys = grad_keys + contract(grad_scores, queries, 0, 0)
    grad_values = grad_values + contract(probs.astype(jnp.bfloat16), grad_rows, 0, 0)
    return (jnp.concatenate(grad_queries, axis=0), grad_keys, grad_values)


def local(tokens, lengths, attn_weights, vectors, up_weights, down_weights, cotangent):
    attn_full, vector_full = (
        lax.all_gather(attn_weights, ("fsdp", "rep"), axis=0, tiled=True),
        lax.all_gather(vectors, ("fsdp", "rep"), axis=0, tiled=True),
    )
    params = vector_full.astype(jnp.float32)
    slot_count, model_width = tokens.shape
    span_rows = min(512, slot_count)
    gain_one = params[0:model_width]
    shift_one = params[model_width : 2 * model_width]
    query_bias = params[2 * model_width : 3 * model_width]
    value_bias = params[3 * model_width : 4 * model_width]
    out_bias = params[4 * model_width : 5 * model_width]
    gain_two = params[5 * model_width : 6 * model_width]
    shift_two = params[6 * model_width : 7 * model_width]
    up_bias = params[7 * model_width : 7 * model_width + FF]
    down_bias = params[7 * model_width + FF :]
    seq_ends = jnp.cumsum(lengths[0])
    positions = lax.iota(jnp.int32, slot_count)
    segment = jnp.sum((positions[:, None] >= seq_ends[None, :]).astype(jnp.int32), axis=1)
    live_rows = (positions < seq_ends[-1]).astype(jnp.float32)[:, None]
    inputs = tokens.astype(jnp.float32)
    normed_one, scaled_one = normalize(inputs)
    hidden_one = (normed_one * gain_one + shift_one).astype(jnp.bfloat16)
    qkv_bias = jnp.concatenate([query_bias, jnp.zeros_like(query_bias), value_bias])
    projected = (contract(hidden_one, attn_full[: 3 * model_width], 1, 1) + qkv_bias).astype(
        jnp.bfloat16
    )
    queries = split_heads(projected[:, :model_width])
    key_heads = split_heads(projected[:, model_width : 2 * model_width])
    value_heads = split_heads(projected[:, 2 * model_width :])

    def attend_forward(head_parts):
        return head_forward(head_parts, segment, span_rows)

    mixed_heads, totals = lax.map(attend_forward, (queries, key_heads, value_heads))
    mixed = join_heads(mixed_heads)
    attended = contract(mixed, attn_full[3 * model_width :], 1, 1) + out_bias
    residual = inputs + attended
    normed_two, scaled_two = normalize(residual)
    hidden_two = (normed_two * gain_two + shift_two).astype(jnp.bfloat16)
    up_full, down_full = (
        lax.all_gather(up_weights, ("fsdp", "rep"), axis=0, tiled=True),
        lax.all_gather(down_weights, ("fsdp", "rep"), axis=0, tiled=True),
    )
    upward = contract(hidden_two, up_full, 1, 1) + up_bias
    activated = jax.nn.gelu(upward, approximate=False).astype(jnp.bfloat16)
    output = (residual + contract(activated, down_full, 1, 0) + down_bias) * live_rows
    up_back, down_back = (
        lax.all_gather(up_weights, ("fsdp", "rep"), axis=0, tiled=True),
        lax.all_gather(down_weights, ("fsdp", "rep"), axis=0, tiled=True),
    )
    grad_output = cotangent.astype(jnp.float32) * live_rows
    grad_down_in = grad_output.astype(jnp.bfloat16)
    grad_down_bias = jnp.sum(grad_down_in.astype(jnp.float32), axis=0)
    grad_act = contract(grad_down_in, down_back, 1, 1)

    def gelu_exact(values):
        return jax.nn.gelu(values, approximate=False)

    grad_upward = jax.vjp(gelu_exact, upward)[1](grad_act)[0]
    grad_up_in = grad_upward.astype(jnp.bfloat16)
    grad_up_bias = jnp.sum(grad_up_in.astype(jnp.float32), axis=0)
    grad_hidden_two = contract(grad_up_in, up_back, 1, 0)
    grad_gain_two = jnp.sum(grad_hidden_two * normed_two, axis=0)
    grad_shift_two = jnp.sum(grad_hidden_two, axis=0)
    grad_residual = grad_output + norm_back(grad_hidden_two, normed_two, scaled_two, gain_two)
    grad_attended = grad_residual.astype(jnp.bfloat16)
    attn_back = lax.all_gather(attn_weights, ("fsdp", "rep"), axis=0, tiled=True)
    grad_out_bias = jnp.sum(grad_attended.astype(jnp.float32), axis=0)
    grad_mixed = contract(grad_attended, attn_back[3 * model_width :], 1, 0).astype(jnp.bfloat16)

    def attend_backward(head_parts):
        return head_backward(head_parts, segment, span_rows)

    grad_q_heads, grad_k_heads, grad_v_heads = lax.map(
        attend_backward, (queries, key_heads, value_heads, totals, split_heads(grad_mixed))
    )
    grad_projected = jnp.concatenate(
        [join_heads(grad_q_heads), join_heads(grad_k_heads), join_heads(grad_v_heads)], axis=1
    ).astype(jnp.bfloat16)
    bias_sums = jnp.sum(grad_projected.astype(jnp.float32), axis=0)
    grad_hidden_one = contract(grad_projected, attn_back[: 3 * model_width], 1, 0)
    grad_gain_one = jnp.sum(grad_hidden_one * normed_one, axis=0)
    grad_shift_one = jnp.sum(grad_hidden_one, axis=0)
    grad_inputs = grad_residual + norm_back(grad_hidden_one, normed_one, scaled_one, gain_one)
    outer_count = lax.axis_size("fsdp")
    inner_count = lax.axis_size("rep")
    inner_index = lax.axis_index("rep")
    attn_left = jnp.concatenate([grad_projected, grad_attended], axis=1)
    attn_block = attn_left.shape[1] // (outer_count * inner_count)
    unit_block = grad_up_in.shape[1] // (outer_count * inner_count)
    bundle = jnp.concatenate(
        [
            by_owner(attn_left, outer_count, inner_count),
            by_owner(grad_up_in, outer_count, inner_count),
            by_owner(activated, outer_count, inner_count),
        ],
        axis=3,
    )
    bundle_width = bundle.shape[3]
    bundle = bundle.reshape(slot_count, inner_count * outer_count * bundle_width)
    received = lax.all_to_all(bundle, "rep", split_axis=1, concat_axis=0, tiled=True)
    received = received.reshape(received.shape[0], outer_count, bundle_width)
    attn_cols = received[:, :, :attn_block].reshape(received.shape[0], outer_count * attn_block)
    up_cols = received[:, :, attn_block : attn_block + unit_block].reshape(
        received.shape[0], outer_count * unit_block
    )
    act_cols = received[:, :, attn_block + unit_block :].reshape(
        received.shape[0], outer_count * unit_block
    )
    outer_ids = lax.iota(jnp.int32, outer_count)[:, None]
    inner_ids = lax.iota(jnp.int32, attn_block)[None, :]
    feature_ids = ((outer_ids * inner_count + inner_index) * attn_block + inner_ids).reshape(
        outer_count * attn_block
    )
    is_projection = (feature_ids < 3 * model_width)[None, :]
    start_sums = (
        jnp.zeros((outer_count * attn_block, model_width), jnp.float32),
        jnp.zeros((outer_count * unit_block, model_width), jnp.float32),
        jnp.zeros((outer_count * unit_block, model_width), jnp.float32),
    )
    piece_h1 = lax.all_gather(hidden_one, "rep", axis=0, tiled=True)
    piece_mixed = lax.all_gather(for_sending(mixed), "rep", axis=0, tiled=True)
    piece_h2 = lax.all_gather(hidden_two, "rep", axis=0, tiled=True)
    piece_dd = lax.all_gather(grad_down_in, "rep", axis=0, tiled=True)
    zero_low = jnp.zeros_like(attn_cols)
    left_proj = jnp.where(is_projection, attn_cols, zero_low)
    left_out = jnp.where(is_projection, zero_low, attn_cols)
    attn_total = (
        start_sums[0] + contract(left_proj, piece_h1, 0, 0) + contract(left_out, piece_mixed, 0, 0)
    )
    up_total = start_sums[1] + contract(up_cols, piece_h2, 0, 0)
    down_total = start_sums[2] + contract(act_cols, piece_dd, 0, 0)
    attn_shard, up_shard, down_shard = (
        lax.psum_scatter(attn_total, "fsdp", scatter_dimension=0, tiled=True),
        lax.psum_scatter(up_total, "fsdp", scatter_dimension=0, tiled=True),
        lax.psum_scatter(down_total, "fsdp", scatter_dimension=0, tiled=True),
    )
    grad_params = jnp.concatenate(
        [
            grad_gain_one,
            grad_shift_one,
            bias_sums[:model_width],
            bias_sums[2 * model_width :],
            grad_out_bias,
            grad_gain_two,
            grad_shift_two,
            grad_up_bias,
            grad_down_bias,
        ]
    )
    vector_shard = lax.psum_scatter(grad_params, ("fsdp", "rep"), scatter_dimension=0, tiled=True)
    return (
        output.astype(jnp.bfloat16),
        grad_inputs.astype(jnp.bfloat16),
        attn_shard,
        vector_shard,
        up_shard,
        down_shard,
    )


def solution(mesh):
    return jax.shard_map(
        local,
        mesh=mesh,
        in_specs=(
            P(("fsdp", "rep"), None),
            P(("fsdp", "rep"), None),
            P(("fsdp", "rep"), None),
            P(("fsdp", "rep")),
            P(("fsdp", "rep"), None),
            P(("fsdp", "rep"), None),
            P(("fsdp", "rep"), None),
        ),
        out_specs=(
            P(("fsdp", "rep"), None),
            P(("fsdp", "rep"), None),
            P(("fsdp", "rep"), None),
            P(("fsdp", "rep")),
            P(("fsdp", "rep"), None),
            P(("fsdp", "rep"), None),
        ),
        check_vma=False,
    )
```

profile of v0, /device:TPU:0, one launch (start us, length us, event | category | flops | bytes accessed | tf_op | source)
XLA Modules:
  0.0 895.3 jit_solution(2756972596517927532)
XLA Ops:
  10.4 42.8 %all-reduce = bf16[13056]{0:T(1024)(128)(2,1)S(1)} all-reduce(bf16[13056]{0:T(1024)(128)(2,1)S(1)} %dynamic-update-slice), channel_id=1, replica_groups=mesh['fsdp'=8,'rep'=4] {'fsdp','rep'}, use_global_device_ids=true, to_apply=%add | all-reduce | flops 13056 | bytes 52224
  56.5 42.6 %all-gather.8.cloned.1.call-done = bf16[4352,1088]{1,0:T(8,128)(2,1)} async-done(((bf16[136,1088]{1,0:T(8,128)(2,1)}), bf16[4352,1088]{1,0:T(8,128)(2,1)}) %all-gather.8.cloned.1.call-update) | async-done | bytes 9469968 | tf_op jit(solution)/shard_map/all_gather | solution.py:94
  99.2 5.5 fusion.50
  108.4 37.9 %while.26 = (s32[]{:T(128)}, bf16[17,256,64]{1,2,0:T(8,128)(2,1)S(1)}, f32[17,256,1]{1,2,0:T(1,128)S(1)}, s32[256]{0:T(256)S(1)}, bf16[17,256,64]{2,1,0:T(8,128)...) while((s32[]{:T(128)}, bf16[17,256,64]{1,2,0:T(8,128)(2,1)S(1)}, ...), condition=%wide.region_7.8_spmd, body=%wide.region_4.7_spmd.sunk | while | flops 17514240 | bytes 1030233 | solution.py:127
  146.4 3.2 fusion.91
  153.8 31.4 %all-gather.10.cloned.1.call-done = bf16[4352,1088]{1,0:T(8,128)(2,1)} async-done(((bf16[136,1088]{1,0:T(8,128)(2,1)}), bf16[4352,1088]{1,0:T(8,128)(2,1)}) %all-gather.10.cloned.1.call-update) | async-done | bytes 9469968 | tf_op jit(solution)/shard_map/all_gather | solution.py:134
  185.2 10.8 %convolution_add_fusion.1 = f32[256,4352]{1,0:T(8,128)} fusion(bf16[256,1088]{0,1:T(8,128)(2,1)S(1)} %copy-done.11, bf16[4352,1088]{1,0:T(8,128)(2,1)} %all-gather.10.cloned.1.call-done, f32[4352]{0:T(1024)S(1)} %slice.95), kind=kOutput, calls=%fused_computation.61 | convolution fusion | flops 2425421824 | bytes 14500864 | tf_op jit(solution)/shard_map/dot_general | solution.py:18
  196.1 75.4 %all-gather.12.cloned.1.call-done = bf16[4352,1088]{1,0:T(8,128)(2,1)} async-done(((bf16[136,1088]{1,0:T(8,128)(2,1)}), bf16[4352,1088]{1,0:T(8,128)(2,1)}) %all-gather.12.cloned.1.call-update) | async-done | bytes 9469968 | tf_op jit(solution)/shard_map/all_gather | solution.py:135
  271.5 17.2 %convert_reduce_fusion = (f32[4352]{0:T(1024)S(1)}, bf16[256,4352]{1,0:T(8,128)(2,1)S(1)}, f32[256,4352]{1,0:T(8,128)}) fusion(f32[256,4352]{1,0:T(8,128)} %convolution_add_fusion.1, bf16[256,1088]{0,1:T(8,128)(2,1)S(1)} %get-tuple-element.146, bf16[4352,1088]{1,0:T(8,128)(2,1)} %all-gather.12.cloned.1.call-done), kind=kOutput, calls=%fused_computation.69 | convolution fusion | flops 2506747648 | bytes 21185536 | tf_op jit(solution)/shard_map/dot_general | solution.py:18
  288.7 9.0 %multiply_reduce_fusion.1 = (f32[1088]{0:T(1024)S(1)}, f32[256]{0:T(256)S(1)}, f32[256]{0:T(256)S(1)}, f32[1088]{0:T(1024)S(1)}, f32[256,1088]{0,1:T(8,128)S(1)}) fusion(f32[256,1088]{0,1:T(8,128)S(1)} %get-tuple-element.175, f32[256]{0:T(256)S(1)} %add_rsqrt_fusion, f32[256]{0:T(256)S(1)} %broadcast_multiply_fusion.4, f32[1088]{0:T(1024)S(1)} %get-tuple-element.165, ...), kind=kOutput, calls=%fused_computation.117 | convolution fusion | flops 2426811904 | bytes 13943552 | tf_op jit(solution)/shard_map/dot_general | solution.py:18
  298.3 3.1 convolution_convert_fusion.1
  302.2 107.8 %while.27 = (s32[]{:T(128)}, bf16[17,256,64]{1,2,0:T(8,128)(2,1)}, bf16[17,256,64]{1,2,0:T(8,128)(2,1)}, bf16[17,256,64]{1,2,0:T(8,128)(2,1)}, s32[256]{0:T(256)...) while((s32[]{:T(128)}, bf16[17,256,64]{1,2,0:T(8,128)(2,1)}, ...), condition=%wide.region_14.15_spmd, body=%wide.region_12.14_spmd.sunk | while | flops 42794752 | bytes 2633841 | solution.py:167
  304.5 1.7 fusion.146
  306.1 1.7 fusion.145
  312.5 1.7 fusion.145
  317.2 1.7 fusion.146
  318.8 1.7 fusion.145
  325.2 1.7 fusion.145
  329.9 1.7 fusion.146
  331.5 1.7 fusion.145
  336.2 1.6 fusion.146
  337.9 1.7 fusion.145
  342.5 1.7 fusion.146
  344.2 1.7 fusion.145
  348.9 1.6 fusion.146
  350.5 1.7 fusion.145
  356.9 1.7 fusion.145
  363.2 1.7 fusion.145
  367.9 1.7 fusion.146
  369.6 1.7 fusion.145
  375.9 1.7 fusion.145
  380.6 1.7 fusion.146
  382.2 1.7 fusion.145
  386.9 1.6 fusion.146
  388.6 1.7 fusion.145
  393.3 1.7 fusion.146
  394.9 1.7 fusion.145
  401.2 1.7 fusion.145
  405.9 1.7 fusion.146
  407.6 1.7 fusion.145
  410.1 3.1 copy.39
  413.1 5.4 multiply_convert_fusion.1
  418.5 4.1 copy.40
  422.7 1.9 pad_maximum_fusion.1
  425.0 4.1 pad_maximum_fusion
  429.1 3.2 copy.41
  432.2 5.3 all-to-all-start
  438.3 88.6 %all-to-all-done = bf16[256,4,3264]{0,2,1:T(8,128)(2,1)} async-done(((bf16[256,4,3264]{0,2,1:T(8,128)(2,1)}), bf16[256,4,3264]{0,2,1:T(8,128)(2,1)}, u32[]{:S(2)}, u32[]{:S(2)}) %all-to-all-start) | async-done | bytes 6684704 | tf_op jit(solution)/shard_map/all_to_all | solution.py:194
  526.9 27.5 %copy.42 = bf16[4,256,3264]{1,0,2:T(4,128)(2,1)} copy(bf16[4,256,3264]{1,2,0:T(8,128)(2,1)} %bitcast.42) | data formatting | bytes 13369344 | tf_op jit(solution)/shard_map/all_to_all | solution.py:194
  554.4 12.7 %reshape.193 = bf16[1024,8,408]{0,2,1:T(8,128)(2,1)} reshape(bf16[4,256,3264]{1,0,2:T(4,128)(2,1)} %copy.42) | data formatting | bytes 13369344 | tf_op jit(solution)/shard_map/reshape | solution.py:195
  567.1 6.2 fusion.87
  573.3 7.6 fusion.93
  581.1 2.6 bitcast_select_fusion
  583.7 7.8 fusion.92
  591.5 7.4 convolution_add_fusion
  600.5 6.5 fusion.94
  607.0 2.0 convert_reduce_fusion.1
  609.0 8.1 fusion.78
  617.2 40.4 %all-reduce.2 = f32[13056]{0:T(1024)S(1)} all-reduce(f32[13056]{0:T(1024)S(1)} %concatenate.21), channel_id=3, replica_groups=mesh['fsdp'=8,'rep'=4] {'fsdp','rep'}, use_global_device_ids=true, to_apply=%region_26.27.clone | all-reduce | flops 13056 | bytes 104448
  658.2 2.9 fusion.77
  661.2 8.7 fusion.62
  669.9 11.4 %reduce-scatter.12.cloned.1.call-done = f32[136,1088]{1,0:T(8,128)} async-done(((f32[1088,1088]{1,0:T(8,128)}), f32[136,1088]{1,0:T(8,128)}) %reduce-scatter.12.cloned.1.call-update) | async-done | bytes 591888
  681.3 103.6 %reduce-scatter.10.cloned.1.call-done = f32[136,1088]{1,0:T(8,128)} async-done(((f32[1088,1088]{1,0:T(8,128)}), f32[136,1088]{1,0:T(8,128)}) %reduce-scatter.10.cloned.1.call-update) | async-done | bytes 591888
  784.9 103.1 %reduce-scatter.14.cloned.1.call-done = f32[136,1088]{1,0:T(8,128)} async-done(((f32[1088,1088]{1,0:T(8,128)}), f32[136,1088]{1,0:T(8,128)}) %reduce-scatter.14.cloned.1.call-update) | async-done | bytes 591888
  (278 shorter events, 118.0 us)
Async XLA Ops:
  7.2 48.9 %copy-start.2 = (bf16[256,1088]{0,1:T(8,128)(2,1)S(1)}, bf16[256,1088]{0,1:T(8,128)(2,1)}, u32[]{:S(2)}) copy-start(bf16[256,1088]{0,1:T(8,128)(2,1)} %param.11) | copy-start | bytes 1671172
  7.2 48.6 %copy-start.18 = (s32[1,4]{1,0:T(1,128)S(1)}, s32[1,4]{1,0:T(1,128)}, u32[]{:S(2)}) copy-start(s32[1,4]{1,0:T(1,128)} %param.12) | copy-start | bytes 52
  7.2 92.0 %all-gather.8.cloned.1.call-start = ((), (), s32[]{:S(2)}) async-start(), calls=%async_computation.4 | async-start | bytes 10340352 | tf_op jit(solution)/shard_map/all_gather | solution.py:94
  7.9 177.3 %all-gather.10.cloned.1.call-start = ((), (), s32[]{:S(2)}) async-start(), calls=%async_computation.5 | async-start | bytes 10340352 | tf_op jit(solution)/shard_map/all_gather | solution.py:134
  8.7 262.8 %all-gather.12.cloned.1.call-start = ((), (), s32[]{:S(2)}) async-start(), calls=%async_computation.6 | async-start | bytes 10340352 | tf_op jit(solution)/shard_map/all_gather | solution.py:135
  9.4 563.9 %all-gather.18.cloned.1.call-start = ((), (), s32[]{:S(2)}) async-start(), calls=%async_computation.9 | async-start | bytes 2785280 | tf_op jit(solution)/shard_map/all_gather | solution.py:216
  56.4 48.2 %copy-start.13 = (bf16[256,1088]{0,1:T(8,128)(2,1)}, bf16[256,1088]{0,1:T(8,128)(2,1)S(1)}, u32[]{:S(2)}) copy-start(bf16[256,1088]{0,1:T(8,128)(2,1)S(1)} %fusion.72) | copy-start | bytes 1671172
  105.5 2.9 copy-start.16
  146.4 3.2 copy-start.15
  146.4 3.2 copy-start.17
  149.6 3.9 copy-start.4
  151.0 34.2 %copy-start.11 = (bf16[256,1088]{0,1:T(8,128)(2,1)S(1)}, bf16[256,1088]{0,1:T(8,128)(2,1)}, u32[]{:S(2)}) copy-start(bf16[256,1088]{0,1:T(8,128)(2,1)} %add_convert_fusion.1) | copy-start | bytes 1671172
  151.0 432.7 %all-gather.14.cloned.1.call-start = ((), (), s32[]{:S(2)}) async-start(), calls=%async_computation.7 | async-start | bytes 2785280 | tf_op jit(solution)/shard_map/all_gather | solution.py:214
  151.6 439.8 %all-gather.16.cloned.1.call-start = ((), (), s32[]{:S(2)}) async-start(), calls=%async_computation.8 | async-start | bytes 2785280 | tf_op jit(solution)/shard_map/all_gather | solution.py:215
  153.8 117.7 %copy-start.14 = (bf16[256,1088]{0,1:T(8,128)(2,1)}, bf16[256,1088]{0,1:T(8,128)(2,1)S(1)}, u32[]{:S(2)}) copy-start(bf16[256,1088]{0,1:T(8,128)(2,1)S(1)} %get-tuple-element.146) | copy-start | bytes 1671172
  288.7 9.0 %copy-start.12 = (bf16[256,4352]{1,0:T(8,128)(2,1)}, bf16[256,4352]{1,0:T(8,128)(2,1)S(1)}, u32[]{:S(2)}) copy-start(bf16[256,4352]{1,0:T(8,128)(2,1)S(1)} %get-tuple-element.148) | copy-start | bytes 6684676
  297.7 3.7 copy-start.6
  298.3 3.1 copy-start.10
  422.7 2.3 copy-start
  432.2 94.7 %all-to-all-start = ((bf16[256,4,3264]{0,2,1:T(8,128)(2,1)}), bf16[256,4,3264]{0,2,1:T(8,128)(2,1)}, u32[]{:S(2)}, u32[]{:S(2)}) async-start(bf16[256,4,3264]{0,2,1:T(8,128)(2,1)} %bitcast.152), calls=%async_computation | async-start | bytes 13369344 | tf_op jit(solution)/shard_map/all_to_all | solution.py:194
  437.5 161.4 %all-gather.20.cloned.1.call-start = ((), (), s32[]{:S(2)}) async-start(), calls=%async_computation.10 | async-start | bytes 2785280 | tf_op jit(solution)/shard_map/all_gather | solution.py:217
  438.3 243.0 %reduce-scatter.12.cloned.1.call-start = ((), (), s32[]{:S(2)}) async-start(), calls=%async_computation.12 | async-start | bytes 5640192
  580.9 204.0 %reduce-scatter.10.cloned.1.call-start = ((), (), s32[]{:S(2)}) async-start(), calls=%async_computation.11 | async-start | bytes 5640192
  583.7 7.8 copy-start.9
  598.8 1.7 copy-start.8
  598.9 289.1 %reduce-scatter.14.cloned.1.call-start = ((), (), s32[]{:S(2)}) async-start(), calls=%async_computation.13 | async-start | bytes 5640192
  607.0 2.0 copy-start.3
  609.0 49.2 %copy-start.5 = (bf16[256,1088]{0,1:T(8,128)(2,1)S(1)}, bf16[256,1088]{0,1:T(8,128)(2,1)}, u32[]{:S(2)}) copy-start(bf16[256,1088]{0,1:T(8,128)(2,1)} %param.17) | copy-start | bytes 1671172
  609.0 49.2 %copy-start.7 = (f32[256,1088]{0,1:T(8,128)S(1)}, f32[256,1088]{0,1:T(8,128)}, u32[]{:S(2)}) copy-start(f32[256,1088]{0,1:T(8,128)} %copy-done.6) | copy-start | bytes 3342340
  658.2 3.0 copy-start.1
Sparse Core Ops, SparseCore 0:
  10.9 88.1 all-gather.7
  102.1 83.1 all-gather.9
  188.2 83.2 all-gather.11
  273.4 22.1 all-gather.17
  297.6 23.5 all-gather.13
  422.8 24.7 all-gather.15
  449.2 37.3 all-gather.19
  581.0 100.2 reduce-scatter.11
  686.0 98.9 reduce-scatter.9
  789.0 98.9 reduce-scatter.13
where the time goes:
time: 907 us; the launch traced here: 895 us
  waiting for transfers between devices  460 us (51%)
  matrix products  237 us (26%)
  blocking collectives  83.2 us (9%)
  local copies, waits for them, and re-layouts  66.3 us (7%)
  other arithmetic  27 us (3%)
  between operations  15.1 us (2%)
    dot_general x131, matrix products, contract(): lax.dot_general(left, right, (((left_dim,), (right_dim,)), ((), ())), pre...  237 us
    unnamed x13, waiting for transfers between devices  222 us
    all_to_all x1, waiting for transfers between devices, local(): lax.all_to_all(bundle, 'rep', split_axis=1, concat_axis=0, tiled=True)  88.6 us
    unnamed x2, blocking collectives  83.2 us
    all_gather x1, waiting for transfers between devices, local(): lax.all_gather(down_weights, ('fsdp', 'rep'), axis=0, tiled=True)  75.4 us
    all_gather x1, waiting for transfers between devices, local(): lax.all_gather(attn_weights, ('fsdp', 'rep'), axis=0, tiled=True)  42.6 us
    all_gather x1, waiting for transfers between devices, local(): lax.all_gather(up_weights, ('fsdp', 'rep'), axis=0, tiled=True)  31.4 us
    all_to_all x1, local copies, waits for them, and re-layouts, local(): lax.all_to_all(bundle, 'rep', split_axis=1, concat_axis=0, tiled=True)  27.5 us
  transfers between devices with their start and end apart: 11, of which 7 were waited for; matrix products, arithmetic and copies ran while one was open for 37% of the time, Pallas kernels for 0%

commit v1 on v0

--- a/solution.py
+++ b/solution.py
@@ -191,7 +191,19 @@
     )
     bundle_width = bundle.shape[3]
     bundle = bundle.reshape(slot_count, inner_count * outer_count * bundle_width)
-    received = lax.all_to_all(bundle, "rep", split_axis=1, concat_axis=0, tiled=True)
+    ways, here = (lax.axis_size("rep"), lax.axis_index("rep"))
+    width_2 = bundle.shape[1] // ways
+    shape = list(bundle.shape)
+    shape[1] = width_2
+    height = shape[0]
+    shape[0] = height * ways
+    full = jnp.zeros(shape, bundle.dtype)
+    for mask in range(ways):
+        part = lax.dynamic_slice_in_dim(bundle, (here ^ mask) * width_2, width_2, axis=1)
+        if mask:
+            part = lax.ppermute(part, "rep", [(d, d ^ mask) for d in range(ways)])
+        full = lax.dynamic_update_slice_in_dim(full, part, (here ^ mask) * height, axis=0)
+    received = full
     received = received.reshape(received.shape[0], outer_count, bundle_width)
     attn_cols = received[:, :, :attn_block].reshape(received.shape[0], outer_count * attn_block)
     up_cols = received[:, :, attn_block : attn_block + unit_block].reshape(

time: 907 us -> 849 us (0.936)
  local copies, waits for them, and re-layouts: 66.3 us -> 39.1 us
  waiting for transfers between devices: 460 us -> 449 us
  matrix products: 237 us -> 227 us
    all_to_all x1 -> x0, waiting for transfers between devices: 88.6 us -> none  [local(): lax.all_to_all(bundle, 'rep', split_axis=1, concat_axis=0, tiled=True)]
    ppermute x0 -> x3, waiting for transfers between devices: none -> 79.8 us  [local(): part = lax.ppermute(part, 'rep', [(d, d ^ mask) for d in range(ways)])]
    all_to_all x1 -> x0, local copies, waits for them, and re-layouts: 27.5 us -> none  [local(): lax.all_to_all(bundle, 'rep', split_axis=1, concat_axis=0, tiled=True)]
    reshape x1 -> x0, local copies, waits for them, and re-layouts: 12.7 us -> none  [local(): received = received.reshape(received.shape[0], outer_count, bundle_width)]
    dot_general x131, matrix products: 237 us -> 227 us  [contract(): lax.dot_general(left, right, (((left_dim,), (right_dim,)), ((), ())), pre...]
  transfers between devices with their start and end apart: 11 -> 13, of which waited for: 7 -> 9; matrix products, arithmetic and copies ran while one was open for 37% -> 34% of each run, Pallas kernels for 0% -> 0%
where the time goes in v1:
time: 849 us; the launch traced here: 841 us
  waiting for transfers between devices  449 us (53%)
  matrix products  227 us (27%)
  blocking collectives  82.5 us (10%)
  local copies, waits for them, and re-layouts  39.1 us (5%)
  other arithmetic  24.5 us (3%)
  between operations  14.9 us (2%)
    dot_general x131, matrix products, contract(): lax.dot_general(left, right, (((left_dim,), (right_dim,)), ((), ())), pre...  227 us
    unnamed x13, waiting for transfers between devices  220 us
    unnamed x2, blocking collectives  82.5 us
    ppermute x3, waiting for transfers between devices, local(): part = lax.ppermute(part, 'rep', [(d, d ^ mask) for d in range(ways)])  79.8 us
    all_gather x1, waiting for transfers between devices, local(): lax.all_gather(down_weights, ('fsdp', 'rep'), axis=0, tiled=True)  75.4 us
    all_gather x1, waiting for transfers between devices, local(): lax.all_gather(attn_weights, ('fsdp', 'rep'), axis=0, tiled=True)  39.7 us
    all_gather x1, waiting for transfers between devices, local(): lax.all_gather(up_weights, ('fsdp', 'rep'), axis=0, tiled=True)  34.4 us
  transfers between devices with their start and end apart: 13, of which 9 were waited for; matrix products, arithmetic and copies ran while one was open for 34% of the time, Pallas kernels for 0%

profile of v1, /device:TPU:0, one launch (start us, length us, event | category | flops | bytes accessed | tf_op | source)
XLA Modules:
  0.0 841.4 jit_solution(13127074362082883518)
XLA Ops:
  11.5 2.0 convert_reduce_fusion.3
  13.9 42.8 %all-reduce = bf16[13056]{0:T(1024)(128)(2,1)S(1)} all-reduce(bf16[13056]{0:T(1024)(128)(2,1)S(1)} %dynamic-update-slice), channel_id=1, replica_groups=mesh['fsdp'=8,'rep'=4] {'fsdp','rep'}, use_global_device_ids=true, to_apply=%add | all-reduce | flops 13056 | bytes 52224
  57.1 1.2 fusion.72
  59.1 39.7 %all-gather.8.cloned.1.call-done = bf16[4352,1088]{1,0:T(8,128)(2,1)} async-done(((bf16[136,1088]{1,0:T(8,128)(2,1)}), bf16[4352,1088]{1,0:T(8,128)(2,1)}) %all-gather.8.cloned.1.call-update) | async-done | bytes 9469968 | tf_op jit(solution)/shard_map/all_gather | solution.py:94
  98.8 5.5 fusion.50
  104.4 1.4 copy.33
  105.9 1.5 copy.34
  107.3 1.4 copy.35
  108.8 38.6 %while.26 = (s32[]{:T(128)}, bf16[17,256,64]{1,2,0:T(8,128)(2,1)S(1)}, f32[17,256,1]{1,2,0:T(1,128)S(1)}, s32[256]{0:T(256)S(1)}, bf16[17,256,64]{2,1,0:T(8,128)...) while((s32[]{:T(128)}, bf16[17,256,64]{1,2,0:T(8,128)(2,1)S(1)}, ...), condition=%wide.region_7.8_spmd, body=%wide.region_4.7_spmd.sunk | while | flops 17514240 | bytes 1030241 | solution.py:127
  126.9 1.2 fusion.133
  147.3 2.8 fusion.91
  150.8 34.4 %all-gather.10.cloned.1.call-done = bf16[4352,1088]{1,0:T(8,128)(2,1)} async-done(((bf16[136,1088]{1,0:T(8,128)(2,1)}), bf16[4352,1088]{1,0:T(8,128)(2,1)}) %all-gather.10.cloned.1.call-update) | async-done | bytes 9469968 | tf_op jit(solution)/shard_map/all_gather | solution.py:134
  185.2 10.8 %convolution_add_fusion.1 = f32[256,4352]{1,0:T(8,128)} fusion(bf16[256,1088]{0,1:T(8,128)(2,1)S(1)} %add_convert_fusion.1, bf16[4352,1088]{1,0:T(8,128)(2,1)} %all-gather.10.cloned.1.call-done, f32[4352]{0:T(1024)S(1)} %slice.95), kind=kOutput, calls=%fused_computation.61 | convolution fusion | flops 2425421824 | bytes 14500864 | tf_op jit(solution)/shard_map/dot_general | solution.py:18
  196.0 75.4 %all-gather.12.cloned.1.call-done = bf16[4352,1088]{1,0:T(8,128)(2,1)} async-done(((bf16[136,1088]{1,0:T(8,128)(2,1)}), bf16[4352,1088]{1,0:T(8,128)(2,1)}) %all-gather.12.cloned.1.call-update) | async-done | bytes 9469968 | tf_op jit(solution)/shard_map/all_gather | solution.py:135
  271.4 17.2 %convert_reduce_fusion = (f32[4352]{0:T(1024)S(1)}, bf16[256,4352]{1,0:T(8,128)(2,1)S(1)}, f32[256,4352]{1,0:T(8,128)}) fusion(f32[256,4352]{1,0:T(8,128)} %convolution_add_fusion.1, bf16[256,1088]{0,1:T(8,128)(2,1)S(1)} %copy-done.20, bf16[4352,1088]{1,0:T(8,128)(2,1)} %all-gather.12.cloned.1.call-done), kind=kOutput, calls=%fused_computation.69 | convolution fusion | flops 2506747648 | bytes 21185536 | tf_op jit(solution)/shard_map/dot_general | solution.py:18
  288.6 9.0 %multiply_reduce_fusion.1 = (f32[1088]{0:T(1024)S(1)}, f32[256]{0:T(256)S(1)}, f32[256]{0:T(256)S(1)}, f32[1088]{0:T(1024)S(1)}, f32[256,1088]{0,1:T(8,128)S(1)}) fusion(f32[256,1088]{0,1:T(8,128)S(1)} %get-tuple-element.179, f32[256]{0:T(256)S(1)} %add_rsqrt_fusion, f32[256]{0:T(256)S(1)} %broadcast_multiply_fusion.4, f32[1088]{0:T(1024)S(1)} %get-tuple-element.169, ...), kind=kOutput, calls=%fused_computation.118 | convolution fusion | flops 2426811904 | bytes 13943552 | tf_op jit(solution)/shard_map/dot_general | solution.py:18
  298.3 3.1 convolution_convert_fusion.1
  302.2 97.5 %while.27 = (s32[]{:T(128)}, bf16[17,256,64]{1,2,0:T(8,128)(2,1)S(1)}, bf16[17,256,64]{1,2,0:T(8,128)(2,1)}, bf16[17,256,64]{1,2,0:T(8,128)(2,1)}, s32[256]{0:T(...) while((s32[]{:T(128)}, ...), condition=%wide.region_14.15_spmd, body=%wide.region_12.14_spmd.sunk | while | flops 42794752 | bytes 2633849 | solution.py:167
  303.2 1.1 multiply_reduce_fusion.7
  305.5 1.6 fusion.146
  311.2 1.6 fusion.146
  317.0 1.7 fusion.146
  322.7 1.6 fusion.146
  328.4 1.7 fusion.146
  334.2 1.6 fusion.146
  339.9 1.7 fusion.146
  345.6 1.6 fusion.146
  351.4 1.6 fusion.146
  357.1 1.6 fusion.146
  362.8 1.7 fusion.146
  368.6 1.6 fusion.146
  374.3 1.7 fusion.146
  380.0 1.6 fusion.146
  385.8 1.7 fusion.146
  391.5 1.6 fusion.146
  397.2 1.7 fusion.146
  400.5 4.1 multiply_convert_fusion.1
  404.6 4.6 copy.37
  409.3 2.5 copy.38
  411.7 1.9 pad_maximum_fusion.1
  414.7 4.1 pad_maximum_fusion
  420.1 2.4 constant_dynamic-slice_fusion.1
  422.6 2.8 copy-done
  425.6 1.6 collective-permute-start.1
  427.6 1.6 collective-permute-done
  429.3 2.9 constant_dynamic-update-slice_fusion.2
  432.1 45.0 %collective-permute-done.1 = bf16[256,3264]{0,1:T(8,128)(2,1)S(1)} collective-permute-done((bf16[256,3264]{0,1:T(8,128)(2,1)}, bf16[256,3264]{0,1:T(8,128)(2,1)S(1)}, u32[]{:S(2)}, u32[]{:S(2)}) %collective-permute-start.1) | collective-permute-done | bytes 1671200 | tf_op jit(solution)/shard_map/ppermute | solution.py:204
  477.1 1.4 constant_dynamic-update-slice_fusion.1
  478.5 33.2 %collective-permute-done.2 = bf16[256,3264]{0,1:T(8,128)(2,1)} collective-permute-done((bf16[256,3264]{0,1:T(8,128)(2,1)}, bf16[256,3264]{0,1:T(8,128)(2,1)}, u32[]{:S(2)}, u32[]{:S(2)}) %collective-permute-start.2) | collective-permute-done | bytes 1671200 | tf_op jit(solution)/shard_map/ppermute | solution.py:204
  511.7 2.8 constant_dynamic-update-slice_fusion.3
  514.5 6.1 fusion.87
  520.7 7.6 fusion.94
  528.5 2.6 bitcast_select_fusion
  531.1 7.8 fusion.92
  538.9 7.1 convolution_add_fusion
  546.3 1.3 copy-done.11
  547.6 6.5 fusion.93
  556.2 8.3 fusion.78
  564.5 39.7 %all-reduce.2 = f32[13056]{0:T(1024)S(1)} all-reduce(f32[13056]{0:T(1024)S(1)} %concatenate.21), channel_id=3, replica_groups=mesh['fsdp'=8,'rep'=4] {'fsdp','rep'}, use_global_device_ids=true, to_apply=%region_26.27.clone | all-reduce | flops 13056 | bytes 104448
  604.9 2.9 fusion.77
  607.9 8.7 %fusion.62 = bf16[256,1088]{0,1:T(8,128)(2,1)} fusion(f32[256,1088]{0,1:T(8,128)S(1)} %get-tuple-element.179, bf16[256,4352]{1,0:T(8,128)(2,1)S(1)} %copy-done.4, bf16[4352,1088]{1,0:T(8,128)(2,1)} %all-gather.12.cloned.1.call-done, f32[256]{0:T(256)S(1)} %compare_convert_fusion, f32[1088]{0:T(1024)S(1)} %get-tuple-element.168), kind=kOutput, calls=%fused_computation.91 | convolution fusion | flops 2425421824 | bytes 13374720 | tf_op jit(solution)/shard_map/dot_general | solution.py:18
  616.5 11.1 %reduce-scatter.14.cloned.1.call-done = f32[136,1088]{1,0:T(8,128)} async-done(((f32[1088,1088]{1,0:T(8,128)}), f32[136,1088]{1,0:T(8,128)}) %reduce-scatter.14.cloned.1.call-update) | async-done | bytes 591888
  627.6 103.6 %reduce-scatter.10.cloned.1.call-done = f32[136,1088]{1,0:T(8,128)} async-done(((f32[1088,1088]{1,0:T(8,128)}), f32[136,1088]{1,0:T(8,128)}) %reduce-scatter.10.cloned.1.call-update) | async-done | bytes 591888
  731.2 103.1 %reduce-scatter.12.cloned.1.call-done = f32[136,1088]{1,0:T(8,128)} async-done(((f32[1088,1088]{1,0:T(8,128)}), f32[136,1088]{1,0:T(8,128)}) %reduce-scatter.12.cloned.1.call-update) | async-done | bytes 591888
  (293 shorter events, 119.8 us)
Async XLA Ops:
  7.2 6.4 copy-start.22
  7.2 49.5 %copy-start.5 = (bf16[256,1088]{0,1:T(8,128)(2,1)S(1)}, bf16[256,1088]{0,1:T(8,128)(2,1)}, u32[]{:S(2)}) copy-start(bf16[256,1088]{0,1:T(8,128)(2,1)} %param.11) | copy-start | bytes 1671172
  7.2 91.6 %all-gather.8.cloned.1.call-start = ((), (), s32[]{:S(2)}) async-start(), calls=%async_computation.3 | async-start | bytes 10340352 | tf_op jit(solution)/shard_map/all_gather | solution.py:94
  7.9 177.3 %all-gather.10.cloned.1.call-start = ((), (), s32[]{:S(2)}) async-start(), calls=%async_computation.4 | async-start | bytes 10340352 | tf_op jit(solution)/shard_map/all_gather | solution.py:134
  8.7 262.7 %all-gather.12.cloned.1.call-start = ((), (), s32[]{:S(2)}) async-start(), calls=%async_computation.5 | async-start | bytes 10340352 | tf_op jit(solution)/shard_map/all_gather | solution.py:135
  9.4 511.3 %all-gather.20.cloned.1.call-start = ((), (), s32[]{:S(2)}) async-start(), calls=%async_computation.9 | async-start | bytes 2785280 | tf_op jit(solution)/shard_map/all_gather | solution.py:229
  13.5 517.6 %all-gather.14.cloned.1.call-start = ((), (), s32[]{:S(2)}) async-start(), calls=%async_computation.6 | async-start | bytes 2785280 | tf_op jit(solution)/shard_map/all_gather | solution.py:226
  58.3 480.6 %all-gather.16.cloned.1.call-start = ((), (), s32[]{:S(2)}) async-start(), calls=%async_computation.7 | async-start | bytes 2785280 | tf_op jit(solution)/shard_map/all_gather | solution.py:227
  147.3 2.8 copy-start.21
  150.7 45.3 %copy-start.18 = (bf16[256,1088]{0,1:T(8,128)(2,1)}, bf16[256,1088]{0,1:T(8,128)(2,1)S(1)}, u32[]{:S(2)}) copy-start(bf16[256,1088]{0,1:T(8,128)(2,1)S(1)} %add_convert_fusion.1) | copy-start | bytes 1671172
  150.7 120.6 %copy-start.20 = (bf16[256,1088]{0,1:T(8,128)(2,1)S(1)}, bf16[256,1088]{0,1:T(8,128)(2,1)}, u32[]{:S(2)}) copy-start(bf16[256,1088]{0,1:T(8,128)(2,1)} %get-tuple-element.146) | copy-start | bytes 1671172
  288.6 9.0 %copy-start.19 = (bf16[256,4352]{1,0:T(8,128)(2,1)}, bf16[256,4352]{1,0:T(8,128)(2,1)S(1)}, u32[]{:S(2)}) copy-start(bf16[256,4352]{1,0:T(8,128)(2,1)S(1)} %get-tuple-element.148) | copy-start | bytes 6684676
  288.6 9.1 %copy-start.7 = (bf16[256,1088]{0,1:T(8,128)(2,1)S(1)}, bf16[256,1088]{0,1:T(8,128)(2,1)}, u32[]{:S(2)}) copy-start(bf16[256,1088]{0,1:T(8,128)(2,1)} %param.17) | copy-start | bytes 1671172
  297.6 3.8 copy-start.9
  298.3 3.1 copy-start.17
  399.7 0.8 copy-start.13
  399.7 146.6 %all-gather.18.cloned.1.call-start = ((), (), s32[]{:S(2)}) async-start(), calls=%async_computation.8 | async-start | bytes 2785280 | tf_op jit(solution)/shard_map/all_gather | solution.py:228
  404.6 7.1 copy-start.3
  411.7 2.3 copy-start.1
  411.7 3.0 copy-start.2
  422.6 2.8 copy-start
  425.4 3.9 collective-permute-start
  425.6 51.5 %collective-permute-start.1 = (bf16[256,3264]{0,1:T(8,128)(2,1)}, bf16[256,3264]{0,1:T(8,128)(2,1)S(1)}, u32[]{:S(2)}, u32[]{:S(2)}) collective-permute-start(bf16[256,3264]{0,1:T(8,128)(2,1)} %get-tuple-element.160), channel_id=1, source_target_pairs={{0,2},{1,3},{2,0},{3,1},{4,6},{5,7},{6,4},{7,5},{8,10},{9,11},{10,... | collective-permute-start | bytes 5013512 | tf_op jit(solution)/shard_map/ppermute | solution.py:204
  427.3 200.3 %reduce-scatter.14.cloned.1.call-start = ((), (), s32[]{:S(2)}) async-start(), calls=%async_computation.12 | async-start | bytes 5640192
  427.5 84.2 %collective-permute-start.2 = (bf16[256,3264]{0,1:T(8,128)(2,1)}, bf16[256,3264]{0,1:T(8,128)(2,1)}, u32[]{:S(2)}, u32[]{:S(2)}) collective-permute-start(bf16[256,3264]{0,1:T(8,128)(2,1)} %get-tuple-element.159), channel_id=1, source_target_pairs={{0,3},{1,2},{2,1},{3,0},{4,7},{5,6},{6,5},{7,4},{8,11},{9,10},{10,... | collective-permute-start | bytes 5013512 | tf_op jit(solution)/shard_map/ppermute | solution.py:204
  528.3 202.9 %reduce-scatter.10.cloned.1.call-start = ((), (), s32[]{:S(2)}) async-start(), calls=%async_computation.10 | async-start | bytes 5640192
  531.1 7.8 copy-start.12
  546.0 1.6 copy-start.11
  546.0 288.3 %reduce-scatter.12.cloned.1.call-start = ((), (), s32[]{:S(2)}) async-start(), calls=%async_computation.11 | async-start | bytes 5640192
  554.1 1.1 copy-start.14
  554.1 1.3 copy-start.15
  554.1 1.5 copy-start.16
  554.1 2.1 copy-start.6
  556.1 48.8 %copy-start.8 = (bf16[256,1088]{0,1:T(8,128)(2,1)S(1)}, bf16[256,1088]{0,1:T(8,128)(2,1)}, u32[]{:S(2)}) copy-start(bf16[256,1088]{0,1:T(8,128)(2,1)} %param.17) | copy-start | bytes 1671172
  556.2 48.8 %copy-start.10 = (f32[256,1088]{0,1:T(8,128)S(1)}, f32[256,1088]{0,1:T(8,128)}, u32[]{:S(2)}) copy-start(f32[256,1088]{0,1:T(8,128)} %copy-done.9) | copy-start | bytes 3342340
  604.9 3.0 copy-start.4
Sparse Core Ops, SparseCore 0:
  10.9 87.7 all-gather.7
  101.7 83.4 all-gather.9
  188.1 83.2 all-gather.11
  273.3 22.1 all-gather.19
  297.5 23.5 all-gather.13
  399.8 22.1 all-gather.15
  427.4 34.1 all-gather.17
  528.4 99.1 reduce-scatter.13
  632.3 98.9 reduce-scatter.9
  735.3 98.9 reduce-scatter.11
